TPU v7x, 32 devices: a whole 2x2x4 slice. The times are simulated.
32 devices in a mesh: dp: 16 (over z, y, core), fsdp: 2 (over x).
Axes of the slice: x: 2, y: 2, z: 4, core: 2. Of those that a mesh axis runs over, the one named last changes fastest.
Arguments:
- frames_in: bfloat16 [16, 1024, 1024], P('dp', 'fsdp'), may hold values from -6 to 6
- prefix_len: int32 [16], P('dp'), may hold values from 1 to 512, as said below
- w_qkv: bfloat16 [1024, 3072], P(('dp', 'fsdp')), may hold values from -0.1875 to 0.1875
- w_out: bfloat16 [1024, 1024], P(('dp', 'fsdp')), may hold values from -1.5 to 1.5
- w_up: bfloat16 [1024, 4096], P(('dp', 'fsdp')), may hold values from -0.1875 to 0.1875
- w_down: bfloat16 [4096, 1024], P(('dp', 'fsdp')), may hold values from -0.09375 to 0.09375
- gains: bfloat16 [2, 1024], P(None, ('dp', 'fsdp')), may hold values from 0.25 to 1.75
- shifts: bfloat16 [2, 1024], P(None, ('dp', 'fsdp')), may hold values from -1.796875 to 1.796875
- cotangent: bfloat16 [16, 1024, 1024], P('dp', 'fsdp'), may hold values from -6 to 6
Outputs:
- frames_out: bfloat16 [16, 1024, 1024], P('dp', 'fsdp')
- grad_in: float32 [16, 1024, 1024], P('dp', 'fsdp')
- grad_qkv: float32 [1024, 3072], P(('dp', 'fsdp'))
- grad_out: float32 [1024, 1024], P(('dp', 'fsdp'))
- grad_up: float32 [1024, 4096], P(('dp', 'fsdp'))
- grad_down: float32 [4096, 1024], P(('dp', 'fsdp'))
- grad_gains: float32 [2, 1024], P(None, ('dp', 'fsdp'))
- grad_shifts: float32 [2, 1024], P(None, ('dp', 'fsdp'))
Inputs may be any that keep to these rules, and one draw needn't show every extreme that they name: `prefix_len`: some item's prefix has exactly 512 frames.
All inputs are finite; a program needn't handle non-finite values.
Results may differ from a plain program's by a relative error of at most 0.011.
Values may be sent and summed in bfloat16 or wider, within the bound.
A program may use at most 256 MiB of HBM per device.

v0:
```python
from functools import partial

import jax
import jax.numpy as jnp
from jax import lax
from jax.sharding import PartitionSpec as P

H = 16
HD = 64


EPS = 1e-05


def norm_rows(values, gain, shift):
    center = values - jnp.mean(values, -1, keepdims=True)
    spread = jnp.mean(center * center, -1, keepdims=True)
    return center * lax.rsqrt(spread + EPS) * gain + shift


def collect(w_qkv, w_out, w_up, w_down, gains, shifts):
    return (
        lax.all_gather(w_qkv, ("dp", "fsdp"), axis=0, tiled=True),
        lax.all_gather(w_out, ("dp", "fsdp"), axis=0, tiled=True),
        lax.all_gather(w_up, ("dp", "fsdp"), axis=0, tiled=True),
        lax.all_gather(w_down, ("dp", "fsdp"), axis=0, tiled=True),
        lax.all_gather(gains, ("dp", "fsdp"), axis=1, tiled=True),
        lax.all_gather(shifts, ("dp", "fsdp"), axis=1, tiled=True),
    )


def split_heads(matrix):
    return matrix.reshape(matrix.shape[0], H, HD).transpose(1, 0, 2)


def join_heads(stacked):
    return stacked.transpose(1, 0, 2).reshape(stacked.shape[1], H * HD)


def masked_scores(query_one, key_one, allowed):
    scores = jnp.dot(query_one, key_one.T, preferred_element_type=jnp.float32) * 0.125
    return jnp.where(allowed, scores, -1e30)


def forward(inputs, weights, allowed):
    w_qkv, w_out, w_up, w_down, gains, shifts = weights
    width = inputs.shape[1]
    gain_rows = gains.astype(jnp.float32)
    shift_rows = shifts.astype(jnp.float32)
    normed = norm_rows(inputs, gain_rows[0], shift_rows[0]).astype(jnp.bfloat16)
    mixed = jnp.dot(normed, w_qkv, preferred_element_type=jnp.float32).astype(jnp.bfloat16)
    queries = mixed[:, :width]
    keys_all, values_all = (
        lax.all_gather(mixed[:, width : 2 * width], "fsdp", axis=0, tiled=True),
        lax.all_gather(mixed[:, 2 * width :], "fsdp", axis=0, tiled=True),
    )
    query_heads = split_heads(queries)
    key_heads = split_heads(keys_all)
    value_heads = split_heads(values_all)

    def single(pieces):
        scores = masked_scores(pieces[0], pieces[1], allowed)
        peak_row = jnp.max(scores, -1, keepdims=True)
        log_total = peak_row + jnp.log(jnp.sum(jnp.exp(scores - peak_row), -1, keepdims=True))
        chance = jnp.exp(scores - log_total).astype(jnp.bfloat16)
        return (jnp.dot(chance, pieces[2], preferred_element_type=jnp.float32), log_total[:, 0])

    outputs, totals = lax.map(single, (query_heads, key_heads, value_heads))
    attended = join_heads(outputs).astype(jnp.bfloat16)
    middle = inputs + jnp.dot(attended, w_out, preferred_element_type=jnp.float32)
    normed_two = norm_rows(middle, gain_rows[1], shift_rows[1]).astype(jnp.bfloat16)
    hidden = jnp.dot(normed_two, w_up, preferred_element_type=jnp.float32)
    active = jax.nn.gelu(hidden, approximate=False).astype(jnp.bfloat16)
    result = middle + jnp.dot(active, w_down, preferred_element_type=jnp.float32)
    saved = (
        normed,
        query_heads,
        key_heads,
        value_heads,
        totals,
        attended,
        middle,
        normed_two,
        hidden,
        active,
    )
    return (result, saved)


def on_device(frames_in, prefix_len, w_qkv, w_out, w_up, w_down, gains, shifts, cotangent):
    inputs = frames_in[0].astype(jnp.float32)
    rows_here = inputs.shape[0]
    frames_all = rows_here * lax.axis_size("fsdp")
    first_row = lax.axis_index("fsdp") * rows_here
    places = first_row + jnp.arange(rows_here, dtype=jnp.int32)
    columns = jnp.arange(frames_all, dtype=jnp.int32)
    allowed = (columns[None, :] <= places[:, None]) | (columns[None, :] < prefix_len[0])
    weights = collect(w_qkv, w_out, w_up, w_down, gains, shifts)
    result, saved = forward(inputs, weights, allowed)
    weights = collect(w_qkv, w_out, w_up, w_down, gains, shifts)
    saved = forward(inputs, weights, allowed)[1]
    full_qkv, full_out, full_up, full_down, full_gains, full_shifts = weights
    (
        normed,
        query_heads,
        key_heads,
        value_heads,
        totals,
        attended,
        middle,
        normed_two,
        hidden,
        active,
    ) = saved
    gain_rows = full_gains.astype(jnp.float32)
    shift_rows = full_shifts.astype(jnp.float32)
    grad_top = cotangent[0].astype(jnp.float32)
    grad_branch = grad_top.astype(jnp.bfloat16)
    part_down = jnp.dot(active.T, grad_branch, preferred_element_type=jnp.float32)
    grad_active = jnp.dot(grad_branch, full_down.T, preferred_element_type=jnp.float32)
    gelu_pull = jax.vjp(partial(jax.nn.gelu, approximate=False), hidden)[1]
    grad_hidden = gelu_pull(grad_active)[0].astype(jnp.bfloat16)
    part_up = jnp.dot(normed_two.T, grad_hidden, preferred_element_type=jnp.float32)
    grad_normed_two = jnp.dot(grad_hidden, full_up.T, preferred_element_type=jnp.float32)
    norm_pull_two = jax.vjp(norm_rows, middle, gain_rows[1], shift_rows[1])[1]
    back_middle, grad_gain_two, grad_shift_two = norm_pull_two(grad_normed_two)
    grad_middle = grad_top + back_middle
    grad_attn_out = grad_middle.astype(jnp.bfloat16)
    part_out = jnp.dot(attended.T, grad_attn_out, preferred_element_type=jnp.float32)
    grad_attended = jnp.dot(grad_attn_out, full_out.T, preferred_element_type=jnp.float32).astype(
        jnp.bfloat16
    )
    grad_att_heads = split_heads(grad_attended)

    def single_back(pieces):
        query_one, key_one, value_one, grad_one, log_total = pieces
        scores = masked_scores(query_one, key_one, allowed)
        chance = jnp.exp(scores - log_total[:, None])
        grad_chance = jnp.dot(grad_one, value_one.T, preferred_element_type=jnp.float32)
        inner = jnp.sum(chance * grad_chance, -1, keepdims=True)
        grad_scores = (chance * (grad_chance - inner)).astype(jnp.bfloat16)
        grad_query = jnp.dot(grad_scores, key_one, preferred_element_type=jnp.float32) * 0.125
        grad_key = (
            jnp.einsum("qk,qd->kd", grad_scores, query_one, preferred_element_type=jnp.float32)
            * 0.125
        )
        grad_value = jnp.einsum(
            "qk,qd->kd", chance.astype(jnp.bfloat16), grad_one, preferred_element_type=jnp.float32
        )
        return (grad_query, grad_key, grad_value)

    grad_q_heads, grad_k_heads, grad_v_heads = lax.map(
        single_back, (query_heads, key_heads, value_heads, grad_att_heads, totals)
    )
    grad_keys, grad_values = (
        lax.psum_scatter(
            join_heads(grad_k_heads).astype(jnp.bfloat16), "fsdp", scatter_dimension=0, tiled=True
        ).astype(jnp.float32),
        lax.psum_scatter(
            join_heads(grad_v_heads).astype(jnp.bfloat16), "fsdp", scatter_dimension=0, tiled=True
        ).astype(jnp.float32),
    )
    grad_mixed = jnp.concatenate([join_heads(grad_q_heads), grad_keys, grad_values], 1).astype(
        jnp.bfloat16
    )
    part_qkv = jnp.dot(normed.T, grad_mixed, preferred_element_type=jnp.float32)
    grad_normed = jnp.dot(grad_mixed, full_qkv.T, preferred_element_type=jnp.float32)
    norm_pull_one = jax.vjp(norm_rows, inputs, gain_rows[0], shift_rows[0])[1]
    back_inputs, grad_gain_one, grad_shift_one = norm_pull_one(grad_normed)
    grad_inputs = grad_middle + back_inputs
    part_gains = jnp.stack([grad_gain_one, grad_gain_two])
    part_shifts = jnp.stack([grad_shift_one, grad_shift_two])
    owned = (
        lax.psum_scatter(part_qkv, ("dp", "fsdp"), scatter_dimension=0, tiled=True),
        lax.psum_scatter(part_out, ("dp", "fsdp"), scatter_dimension=0, tiled=True),
        lax.psum_scatter(part_up, ("dp", "fsdp"), scatter_dimension=0, tiled=True),
        lax.psum_scatter(part_down, ("dp", "fsdp"), scatter_dimension=0, tiled=True),
        lax.psum_scatter(part_gains, ("dp", "fsdp"), scatter_dimension=1, tiled=True),
        lax.psum_scatter(part_shifts, ("dp", "fsdp"), scatter_dimension=1, tiled=True),
    )
    return (
        result.astype(jnp.bfloat16)[None],
        grad_inputs[None],
        owned[0],
        owned[1],
        owned[2],
        owned[3],
        owned[4],
        owned[5],
    )


def solution(mesh):
    placed = (
        P("dp", "fsdp", None),
        P("dp"),
        P(("dp", "fsdp"), None),
        P(("dp", "fsdp"), None),
        P(("dp", "fsdp"), None),
        P(("dp", "fsdp"), None),
        P(None, ("dp", "fsdp")),
        P(None, ("dp", "fsdp")),
        P("dp", "fsdp", None),
    )
    return jax.shard_map(
        on_device,
        mesh=mesh,
        in_specs=placed,
        out_specs=(
            P("dp", "fsdp", None),
            P("dp", "fsdp", None),
            P(("dp", "fsdp"), None),
            P(("dp", "fsdp"), None),
            P(("dp", "fsdp"), None),
            P(("dp", "fsdp"), None),
            P(None, ("dp", "fsdp")),
            P(None, ("dp", "fsdp")),
        ),
        check_vma=False,
    )
```

profile of v0, /device:TPU:0, one launch (start us, length us, event | category | flops | bytes accessed | tf_op | source)
XLA Modules:
  0.0 1990.7 jit_solution(14223216084970158019)
XLA Ops:
  7.9 69.8 %all-gather.1 = bf16[32,32,2]{1,2,0:T(2,128)(2,1)S(1)} all-gather(bf16[1,32,2]{1,2,0:T(2,128)(2,1)} %bitcast.281), channel_id=1, replica_groups=mesh['dp'=16,'fsdp'=2] {'dp','fsdp'}, dimensions={0}, use_global_device_ids=true | all-gather | bytes 4224 | tf_op jit(solution)/shard_map/all_gather | solution.py:28
  77.8 63.1 %all-gather = bf16[32,32,2]{1,2,0:T(2,128)(2,1)S(1)} all-gather(bf16[1,32,2]{1,2,0:T(2,128)(2,1)} %bitcast.282), channel_id=1, replica_groups=mesh['dp'=16,'fsdp'=2] {'dp','fsdp'}, dimensions={0}, use_global_device_ids=true | all-gather | bytes 4224 | tf_op jit(solution)/shard_map/all_gather | solution.py:27
  144.2 6.7 convolution_convert_fusion
  158.4 25.5 %all-gather.11.cloned.1.call-done = bf16[1024,1024]{1,0:T(8,128)(2,1)} async-done(((bf16[512,1024]{1,0:T(8,128)(2,1)}), bf16[1024,1024]{1,0:T(8,128)(2,1)}) %all-gather.11.cloned.1.call-update) | async-done | bytes 2097168 | tf_op jit(solution)/shard_map/all_gather | solution.py:54
  183.9 2.9 copy.56
  186.7 3.2 copy.59
  189.9 29.2 %all-gather.13.cloned.1.call-done = bf16[1024,1024]{1,0:T(8,128)(2,1)} async-done(((bf16[512,1024]{1,0:T(8,128)(2,1)}), bf16[1024,1024]{1,0:T(8,128)(2,1)}) %all-gather.13.cloned.1.call-update) | async-done | bytes 2097168 | tf_op jit(solution)/shard_map/all_gather | solution.py:55
  219.1 2.9 copy.57
  222.0 3.2 copy.60
  225.3 62.7 %while.40 = (s32[]{:T(128)}, bf16[16,512,64]{1,2,0:T(8,128)(2,1)S(1)}, f32[16,512]{1,0:T(8,128)S(1)}, bf16[16,512,64]{2,1,0:T(8,128)(2,1)}, bf16[16,1024,64]{2,1...) while((s32[]{:T(128)}, ...), condition=%wide.region_11.12_spmd.clone, body=%wide.region_8.11_spmd.clone.sunk | while | flops 138935808 | bytes 7101553 | solution.py:68
  288.9 3.3 fusion.155
  292.7 64.9 %all-gather.17.cloned.1.call-done = bf16[1024,4096]{1,0:T(8,128)(2,1)} async-done(((bf16[32,4096]{1,0:T(8,128)(2,1)}), bf16[1024,4096]{1,0:T(8,128)(2,1)}) %all-gather.17.cloned.1.call-update) | async-done | bytes 8388624 | tf_op jit(solution)/shard_map/all_gather | solution.py:25
  357.6 26.2 %fusion.58 = (f32[512,4096]{1,0:T(8,128)}, f32[512,4096]{1,0:T(8,128)}) fusion(bf16[1024,4096]{1,0:T(8,128)(2,1)} %all-gather.17.cloned.1.call-done, f32[512,1024]{1,0:T(8,128)S(1)} %get-tuple-element.357, f32[512]{0:T(512)S(1)} %fusion.108, f32[512]{0:T(512)S(1)} %broadcast_multiply_fusion, f32[1024]{0:T(1024)S(1)} %bitcast.273, f32[1024]{0:T(1024)S(1)} %bitcast.268), kind=kOutput, calls=%fused_computation.77 | convolution fusion | flops 4427612160 | bytes 27275264 | tf_op jit(solution)/shard_map/dot_general | solution.py:72
  383.8 52.7 %all-gather.19.cloned.1.call-done = bf16[4096,1024]{1,0:T(8,128)(2,1)} async-done(((bf16[128,1024]{1,0:T(8,128)(2,1)}), bf16[4096,1024]{1,0:T(8,128)(2,1)}) %all-gather.19.cloned.1.call-update) | async-done | bytes 8388624 | tf_op jit(solution)/shard_map/all_gather | solution.py:26
  436.5 14.7 add_convert_fusion
  451.1 7.0 multiply_reduce_fusion.1
  467.2 153.1 %while.41 = (s32[]{:T(128)}, bf16[16,512,64]{1,2,0:T(8,128)(2,1)}, bf16[16,1024,64]{1,2,0:T(8,128)(2,1)}, bf16[16,1024,64]{1,2,0:T(8,128)(2,1)}, bf16[16,512,64]...) while((s32[]{:T(128)}, bf16[16,512,64]{1,2,0:T(8,128)(2,1)}, ...), condition=%wide.region_18.19_spmd.clone, body=%wide.region_16.18_spmd.clone.sunk | while | flops 341409280 | bytes 17582208 | solution.py:152
  621.2 29.8 %reduce-scatter.15.cloned.1.call-done = bf16[512,1024]{0,1:T(8,128)(2,1)} async-done(((bf16[1024,1024]{0,1:T(8,128)(2,1)}), bf16[512,1024]{0,1:T(8,128)(2,1)}) %reduce-scatter.15.cloned.1.call-update) | async-done | bytes 1048592 | tf_op jit(solution)/shard_map/reduce_scatter | solution.py:159
  651.0 34.8 %reduce-scatter.13.cloned.1.call-done = bf16[512,1024]{0,1:T(8,128)(2,1)} async-done(((bf16[1024,1024]{0,1:T(8,128)(2,1)}), bf16[512,1024]{0,1:T(8,128)(2,1)}) %reduce-scatter.13.cloned.1.call-update) | async-done | bytes 1048592 | tf_op jit(solution)/shard_map/reduce_scatter | solution.py:156
  685.7 7.7 fusion.147
  698.0 4.7 fusion.156
  703.4 10.1 fusion.95
  713.7 10.4 fusion.145
  725.3 14.3 fusion.71
  740.7 71.5 %while.39 = (s32[]{:T(128)}, bf16[16,512,64]{1,2,0:T(8,128)(2,1)}, bf16[16,512,64]{2,1,0:T(8,128)(2,1)}, bf16[16,1024,64]{2,1,0:T(8,128)(2,1)}, bf16[16,1024,64]...) while((s32[]{:T(128)}, bf16[16,512,64]{1,2,0:T(8,128)(2,1)}, ...), condition=%wide.region_5.6_spmd.clone, body=%wide.region_2.5_spmd.clone.sunk | while | flops 138935808 | bytes 7097437 | solution.py:68
  816.2 32.2 %fusion.91 = bf16[1,512,1024]{2,1,0:T(8,128)(2,1)} fusion(f32[512,1024]{1,0:T(8,128)} %copy-done.8, bf16[4096,1024]{1,0:T(8,128)(2,1)} %all-gather.19.cloned.1.call-done, bf16[1024,4096]{1,0:T(8,128)(2,1)} %all-gather.17.cloned.1.call-done, f32[1024]{0:T(1024)S(1)} %bitcast.275, f32[1024]{0:T(1024)S(1)} %bitcast.272, f32[512]{0:T(512)S(1)} %add_rsqrt_fusion, ...), kind=kOutput, calls=%fused_computation.141 | convolution fusion | flops 8729919488 | bytes 19935232 | tf_op jit(solution)/shard_map/dot_general | solution.py:74
  848.4 4.1 add_bitcast_fusion
  853.9 109.6 %reduce-scatter.27.cloned.1.call-done = f32[32,2]{1,0:T(8,128)} async-done(((f32[1024,2]{1,0:T(8,128)}), f32[32,2]{1,0:T(8,128)}) %reduce-scatter.27.cloned.1.call-update) | async-done | bytes 272
  964.8 139.4 %reduce-scatter.19.cloned.1.call-done = f32[32,1024]{1,0:T(8,128)} async-done(((f32[1024,1024]{1,0:T(8,128)}), f32[32,1024]{1,0:T(8,128)}) %reduce-scatter.19.cloned.1.call-update) | async-done | bytes 131088 | tf_op jit(solution)/shard_map/reduce_scatter | solution.py:175
  1104.3 158.8 %reduce-scatter.17.cloned.1.call-done = f32[32,3072]{1,0:T(8,128)} async-done(((f32[1024,3072]{1,0:T(8,128)}), f32[32,3072]{1,0:T(8,128)}) %reduce-scatter.17.cloned.1.call-update) | async-done | bytes 393232 | tf_op jit(solution)/shard_map/reduce_scatter | solution.py:174
  1263.0 359.4 %reduce-scatter.21.cloned.1.call-done = f32[32,4096]{1,0:T(8,128)} async-done(((f32[1024,4096]{1,0:T(8,128)}), f32[32,4096]{1,0:T(8,128)}) %reduce-scatter.21.cloned.1.call-update) | async-done | bytes 524304 | tf_op jit(solution)/shard_map/reduce_scatter | solution.py:176
  1622.5 361.5 %reduce-scatter.23.cloned.1.call-done = f32[128,1024]{1,0:T(8,128)} async-done(((f32[4096,1024]{1,0:T(8,128)}), f32[128,1024]{1,0:T(8,128)}) %reduce-scatter.23.cloned.1.call-update) | async-done | bytes 524304 | tf_op jit(solution)/shard_map/reduce_scatter | solution.py:177
  (366 shorter events, 322.6 us)
Async XLA Ops:
  7.2 137.1 %all-gather.9.cloned.1.call-start = ((), (), s32[]{:S(2)}) async-start(), calls=%async_computation.8 | async-start | bytes 6488064 | tf_op jit(solution)/shard_map/all_gather | solution.py:23
  7.9 176.0 %all-gather.11.cloned.1.call-start = ((), (), s32[]{:S(2)}) async-start(), calls=%async_computation.9 | async-start | bytes 3145728 | tf_op jit(solution)/shard_map/all_gather | solution.py:54
  144.1 6.8 copy-start.13
  144.2 6.7 copy-start.15
  152.6 66.5 %all-gather.13.cloned.1.call-start = ((), (), s32[]{:S(2)}) async-start(), calls=%async_computation.10 | async-start | bytes 3145728 | tf_op jit(solution)/shard_map/all_gather | solution.py:55
  153.4 134.6 %all-gather.15.cloned.1.call-start = ((), (), s32[]{:S(2)}) async-start(), calls=%async_computation.11 | async-start | bytes 2162688 | tf_op jit(solution)/shard_map/all_gather | solution.py:24
  153.9 203.7 %all-gather.17.cloned.1.call-start = ((), (), s32[]{:S(2)}) async-start(), calls=%async_computation.12 | async-start | bytes 8650752 | tf_op jit(solution)/shard_map/all_gather | solution.py:25
  154.5 281.9 %all-gather.19.cloned.1.call-start = ((), (), s32[]{:S(2)}) async-start(), calls=%async_computation.13 | async-start | bytes 8650752 | tf_op jit(solution)/shard_map/all_gather | solution.py:26
  155.1 495.9 %reduce-scatter.15.cloned.1.call-start = ((), (), s32[]{:S(2)}) async-start(), calls=%async_computation.15 | async-start | bytes 3145728 | tf_op jit(solution)/shard_map/reduce_scatter | solution.py:159
  225.3 63.7 %copy-start = (bf16[1,512,1024]{2,1,0:T(8,128)(2,1)S(1)}, bf16[1,512,1024]{2,1,0:T(8,128)(2,1)}, u32[]{:S(2)}) copy-start(bf16[1,512,1024]{2,1,0:T(8,128)(2,1)} %param.15) | copy-start | bytes 3145732
  287.9 1.0 copy-start.9
  436.5 14.7 copy-start.17
  458.1 2.1 copy-start.3
  458.1 3.4 copy-start.6
  458.9 1.4 copy-start.1
  458.9 5.0 copy-start.11
  460.6 1.0 copy-start.10
  620.4 65.3 %reduce-scatter.13.cloned.1.call-start = ((), (), s32[]{:S(2)}) async-start(), calls=%async_computation.14 | async-start | bytes 3145728 | tf_op jit(solution)/shard_map/reduce_scatter | solution.py:156
  621.1 231.5 %reduce-scatter.25.cloned.1.call-start = ((), (), s32[]{:S(2)}) async-start(), calls=%async_computation.20 | async-start | bytes 540672
  685.7 7.8 copy-start.14
  693.5 1.3 copy-start.5
  696.9 266.6 %reduce-scatter.27.cloned.1.call-start = ((), (), s32[]{:S(2)}) async-start(), calls=%async_computation.21 | async-start | bytes 540672
  698.0 406.3 %reduce-scatter.19.cloned.1.call-start = ((), (), s32[]{:S(2)}) async-start(), calls=%async_computation.17 | async-start | bytes 4325376 | tf_op jit(solution)/shard_map/reduce_scatter | solution.py:175
  702.8 0.7 copy-start.16
  702.8 560.2 %reduce-scatter.17.cloned.1.call-start = ((), (), s32[]{:S(2)}) async-start(), calls=%async_computation.16 | async-start | bytes 12976128 | tf_op jit(solution)/shard_map/reduce_scatter | solution.py:174
  713.6 908.9 %reduce-scatter.21.cloned.1.call-start = ((), (), s32[]{:S(2)}) async-start(), calls=%async_computation.18 | async-start | bytes 17301504 | tf_op jit(solution)/shard_map/reduce_scatter | solution.py:176
  724.1 1.2 copy-start.4
  724.1 1259.8 %reduce-scatter.23.cloned.1.call-start = ((), (), s32[]{:S(2)}) async-start(), calls=%async_computation.19 | async-start | bytes 17301504 | tf_op jit(solution)/shard_map/reduce_scatter | solution.py:177
  740.7 71.5 %copy-start.7 = (bf16[1024,1024]{1,0:T(8,128)(2,1)S(1)}, bf16[1024,1024]{1,0:T(8,128)(2,1)}, u32[]{:S(2)}) copy-start(bf16[1024,1024]{1,0:T(8,128)(2,1)} %all-gather.15.cloned.1.call-done) | copy-start | bytes 6291460
  814.8 1.3 copy-start.8
  816.2 32.3 %copy-start.2 = (f32[512,1024]{1,0:T(8,128)S(1)}, f32[512,1024]{1,0:T(8,128)}, u32[]{:S(2)}) copy-start(f32[512,1024]{1,0:T(8,128)} %copy-done.1) | copy-start | bytes 6291460
  816.2 32.3 %copy-start.12 = (f32[512]{0:T(512)S(1)}, f32[512]{0:T(512)}, u32[]{:S(2)}) copy-start(f32[512]{0:T(512)} %copy-done.11) | copy-start | bytes 6148
Sparse Core Ops, SparseCore 0:
  10.9 72.1 all-gather.8
  152.7 31.0 all-gather.10
  186.0 33.1 all-gather.12
  222.0 56.5 all-gather.14
  281.4 76.1 all-gather.16
  360.4 75.9 all-gather.18
  620.5 30.4 reduce-scatter.14
  653.9 31.8 reduce-scatter.12
  697.0 134.2 reduce-scatter.24
  833.4 130.0 reduce-scatter.26
  966.3 137.8 reduce-scatter.18
  1110.7 152.2 reduce-scatter.16
  1266.0 356.4 reduce-scatter.20
  1625.3 358.6 reduce-scatter.22
where the time goes:
time: 2000 us; the launch traced here: 1990 us
  waiting for transfers between devices  1370 us (68%)
  matrix products  407 us (20%)
  blocking collectives  133 us (7%)
  local copies, waits for them, and re-layouts  34.1 us (2%)
  other arithmetic  30.8 us (2%)
    reduce_scatter x1, waiting for transfers between devices, on_device(): lax.psum_scatter(part_down, ('dp', 'fsdp'), scatter_dimension=0, tiled=True)  361 us
    reduce_scatter x1, waiting for transfers between devices, on_device(): lax.psum_scatter(part_up, ('dp', 'fsdp'), scatter_dimension=0, tiled=True)  359 us
    reduce_scatter x1, waiting for transfers between devices, on_device(): lax.psum_scatter(part_qkv, ('dp', 'fsdp'), scatter_dimension=0, tiled=True)  159 us
    reduce_scatter x1, waiting for transfers between devices, on_device(): lax.psum_scatter(part_out, ('dp', 'fsdp'), scatter_dimension=0, tiled=True)  139 us
    unnamed x16, waiting for transfers between devices  113 us
    dot_general x48, matrix products, masked_scores(): jnp.dot(query_one, key_one.T, preferred_element_type=jnp.float32) * 0.125  90.9 us
    all_gather x1, blocking collectives, collect(): lax.all_gather(shifts, ('dp', 'fsdp'), axis=1, tiled=True)  69.8 us
    all_gather x1, waiting for transfers between devices, collect(): lax.all_gather(w_up, ('dp', 'fsdp'), axis=0, tiled=True)  64.9 us
  transfers between devices with their start and end apart: 14, of which 11 were waited for; matrix products, arithmetic and copies ran while one was open for 13% of the time, Pallas kernels for 0%

commit v1 on v0

--- a/solution.py
+++ b/solution.py
@@ -1,15 +1,880 @@
-from functools import partial
+import functools
+import math
 
 import jax
 import jax.numpy as jnp
 from jax import lax
+from jax.experimental import pallas as pl
+from jax.experimental.pallas import tpu as pltpu
 from jax.sharding import PartitionSpec as P
 
 H = 16
 HD = 64
-
-
 EPS = 1e-05
+BF = jnp.bfloat16
+F32 = jnp.float32
+LOG2E = math.log2(math.e)
+SCALE2 = 0.125 * LOG2E
+PAIR = 2 * HD
+TILE = 512
+MESH = pl.DeviceIdType.MESH
+DMA = pltpu.SemaphoreType.DMA
+VMEM_LIMIT = 60 * 2**20
+
+
+def coords():
+    dp, f = lax.axis_index("dp"), lax.axis_index("fsdp")
+    q = lax.div(dp, 2)
+    return lax.div(q, 2), lax.rem(q, 2), lax.rem(dp, 2), f
+
+
+def dev(z, y, c, f):
+    return ((z * 2 + y) * 2 + c, f)
+
+
+def remote(src, dst, send, recv, device):
+    return pltpu.make_async_remote_copy(
+        src_ref=src, dst_ref=dst, send_sem=send, recv_sem=recv, device_id=device, device_id_type=MESH
+    )
+
+
+def greet(peers):
+    barrier = pltpu.get_barrier_semaphore()
+    for peer in peers:
+        pl.semaphore_signal(barrier, inc=1, device_id=peer, device_id_type=MESH)
+    pl.semaphore_wait(barrier, len(peers))
+
+
+def all_peers(nz, z, y, c, f):
+    peers = [dev(lax.rem(z + k, nz), y, c, f) for k in range(1, nz)]
+    return peers + [dev(z, 1 - y, c, f), dev(z, y, c, 1 - f), dev(z, y, 1 - c, f)]
+
+
+def dot_nn(a, b):
+    return lax.dot_general(a, b, (((1,), (0,)), ((), ())), preferred_element_type=F32)
+
+
+def dot_nt(a, b):
+    return lax.dot_general(a, b, (((1,), (1,)), ((), ())), preferred_element_type=F32)
+
+
+def dot_tn(a, b):
+    return lax.dot_general(a, b, (((0,), (0,)), ((), ())), preferred_element_type=F32)
+
+
+def tiles(count, size, body):
+    @pl.loop(0, count)
+    def _(j):
+        body(j, pl.ds(pl.multiple_of(j * size, size), size))
+
+
+def normalise(v):
+    center = v - jnp.mean(v, -1, keepdims=True)
+    scale = lax.rsqrt(jnp.mean(center * center, -1, keepdims=True) + EPS)
+    return center * scale, scale
+
+
+class Gather:
+    def __init__(self, nz, place, shards, outs, sems):
+        self.nz, self.place, self.shards, self.outs = nz, place, shards, outs
+        self.send, self.recv, self.core_send, self.core_recv, self.own = sems
+
+    @staticmethod
+    def sem_shapes(nz, nw):
+        return [DMA((nw, 32)), DMA((nw, 32)), DMA((nw, 4 * nz)), DMA((nw, 4 * nz)), DMA((nw,))]
+
+    def block(self, w, zz, yy, ff):
+        return self.outs[w].at[zz, yy, self.place[2], ff]
+
+    def hop(self, w, src, zz, yy, ff, slot, device):
+        return remote(src, self.block(w, zz, yy, ff), self.send.at[w, slot], self.recv.at[w, slot], device)
+
+    def arrive(self, w, zz, yy, ff, slot):
+        dst = self.block(w, zz, yy, ff)
+        remote(dst, dst, self.send.at[w, slot], self.recv.at[w, slot], self.core()).wait_recv()
+
+    def core(self):
+        z, y, c, f = self.place
+        return dev(z, y, 1 - c, f)
+
+    def to_core(self, w, src, zz, yy, ff, slot):
+        remote(
+            src, self.block(w, zz, yy, ff), self.core_send.at[w, slot], self.core_recv.at[w, slot], self.core()
+        ).start()
+
+    def zk(self, k):
+        return lax.rem(self.place[0] + self.nz - k, self.nz)
+
+    def zt(self, k):
+        return lax.rem(self.place[0] + k, self.nz)
+
+    def e0(self, w):
+        z, y, c, f = self.place
+        nz, mine = self.nz, self.shards[w]
+        pltpu.make_async_copy(mine, self.block(w, z, y, f), self.own.at[w]).start()
+
+        @pl.when(c == 0)
+        def _():
+            for k in range(1, nz):
+                self.hop(w, mine, z, y, f, k - 1, dev(self.zt(k), y, c, f)).start()
+            self.hop(w, mine, z, y, f, 4, dev(z, 1 - y, c, f)).start()
+            self.hop(w, mine, z, y, f, 8, dev(z, y, c, 1 - f)).start()
+
+        @pl.when(c == 1)
+        def _():
+            self.hop(w, mine, z, y, f, 0, dev(z, y, c, 1 - f)).start()
+            for k in range(1, nz):
+                self.hop(w, mine, z, y, f, k, dev(self.zt(k), y, c, f)).start()
+            self.hop(w, mine, z, y, f, 8, dev(z, 1 - y, c, f)).start()
+
+        self.to_core(w, mine, z, y, f, 0)
+
+    def e1(self, w):
+        z, y, c, f = self.place
+        nz = self.nz
+
+        @pl.when(c == 0)
+        def _():
+            for k in range(1, nz):
+                zz = self.zk(k)
+                self.arrive(w, zz, y, f, k - 1)
+                src = self.block(w, zz, y, f)
+                self.hop(w, src, zz, y, f, 4 + k, dev(z, 1 - y, c, f)).start()
+                self.hop(w, src, zz, y, f, 8 + k, dev(z, y, c, 1 - f)).start()
+                self.to_core(w, src, zz, y, f, k)
+
+        @pl.when(c == 1)
+        def _():
+            self.arrive(w, z, y, 1 - f, 0)
+            src = self.block(w, z, y, 1 - f)
+            for k in range(1, nz):
+                self.hop(w, src, z, y, 1 - f, 3 + k, dev(self.zt(k), y, c, f)).start()
+            self.hop(w, src, z, y, 1 - f, 12, dev(z, 1 - y, c, f)).start()
+            self.to_core(w, src, z, y, 1 - f, 4)
+
+    def e2(self, w):
+        z, y, c, f = self.place
+        nz = self.nz
+
+        @pl.when(c == 0)
+        def _():
+            for k in range(nz):
+                zz = self.zk(k)
+                self.arrive(w, zz, 1 - y, f, 4 + k)
+                src = self.block(w, zz, 1 - y, f)
+                self.hop(w, src, zz, 1 - y, f, 12 + k, dev(z, y, c, 1 - f)).start()
+                self.to_core(w, src, zz, 1 - y, f, 4 + k)
+
+        @pl.when(c == 1)
+        def _():
+            for h in range(2):
+                ff = f if h == 0 else 1 - f
+                for k in range(1, nz):
+                    zz = self.zk(k)
+                    self.arrive(w, zz, y, ff, 3 * h + k)
+                    src = self.block(w, zz, y, ff)
+                    self.hop(w, src, zz, y, ff, 8 + 4 * h + k, dev(z, 1 - y, c, f)).start()
+                    self.to_core(w, src, zz, y, ff, 4 * h + k)
+
+    def e3(self, w):
+        z, y, c, f = self.place
+        nz = self.nz
+
+        @pl.when(c == 0)
+        def _():
+            for h in range(2):
+                yy = y if h == 0 else 1 - y
+                for k in range(nz):
+                    zz = self.zk(k)
+                    self.arrive(w, zz, yy, 1 - f, 8 + 4 * h + k)
+                    self.to_core(w, self.block(w, zz, yy, 1 - f), zz, yy, 1 - f, 8 + 4 * h + k)
+
+        @pl.when(c == 1)
+        def _():
+            for h in range(2):
+                ff = f if h == 0 else 1 - f
+                for k in range(nz):
+                    zz = self.zk(k)
+                    self.arrive(w, zz, 1 - y, ff, 8 + 4 * h + k)
+                    self.to_core(w, self.block(w, zz, 1 - y, ff), zz, 1 - y, ff, 8 + 4 * h + k)
+
+    def e4(self, w):
+        z, y, c, f = self.place
+        pltpu.make_async_copy(self.shards[w], self.block(w, z, y, f), self.own.at[w]).wait()
+
+        def from_core(order):
+            for slot, (zz, yy, ff) in enumerate(order):
+                dst = self.outs[w].at[zz, yy, 1 - c, ff]
+                remote(dst, dst, self.core_send.at[w, slot], self.core_recv.at[w, slot], self.core()).wait_recv()
+
+        ks = range(self.nz)
+
+        @pl.when(c == 1)
+        def _():
+            from_core([(self.zk(k), yy, ff) for yy, ff in ((y, f), (1 - y, f), (y, 1 - f), (1 - y, 1 - f)) for k in ks])
+
+        @pl.when(c == 0)
+        def _():
+            from_core([(self.zk(k), yy, ff) for yy, ff in ((y, f), (y, 1 - f), (1 - y, f), (1 - y, 1 - f)) for k in ks])
+
+    def finish(self, w):
+        z, y, c, f = self.place
+        some = self.shards[w]
+
+        def drain(sems, slots):
+            for slot in slots:
+                remote(some, self.block(w, z, y, f), sems.at[w, slot], self.recv.at[w, 0], self.core()).wait_send()
+
+        @pl.when(c == 0)
+        def _():
+            drain(self.send, [k - 1 for k in range(1, self.nz)] + list(range(4, 16)))
+
+        @pl.when(c == 1)
+        def _():
+            drain(self.send, list(range(0, 7)) + list(range(8, 16)))
+
+        drain(self.core_send, range(16))
+
+
+def gather_kernel(nz, nw, *refs):
+    place = coords()
+    g = Gather(nz, place, refs[:nw], refs[nw : 2 * nw], refs[2 * nw :])
+    greet(all_peers(nz, *place))
+    for step in range(nw + 3):
+        for stage, call in enumerate((g.e0, g.e1, g.e2, g.e3)):
+            if 0 <= step - stage < nw:
+                call(step - stage)
+    for w in range(nw):
+        g.e4(w)
+    for w in range(nw):
+        g.finish(w)
+
+
+def gather(nz, shards):
+    nw = len(shards)
+    return pl.pallas_call(
+        functools.partial(gather_kernel, nz, nw),
+        out_shape=[jax.ShapeDtypeStruct((nz, 2, 2, 2) + s.shape, s.dtype) for s in shards],
+        in_specs=[pl.BlockSpec(memory_space=pl.ANY)] * nw,
+        out_specs=[pl.BlockSpec(memory_space=pl.ANY)] * nw,
+        scratch_shapes=Gather.sem_shapes(nz, nw),
+        compiler_params=pltpu.CompilerParams(collective_id=0, has_side_effects=True),
+    )(*shards)
+
+
+def lane_half():
+    return lax.broadcasted_iota(jnp.int32, (1, PAIR), 1) // HD
+
+
+def fill_bias(bias, prefix, c, transposed):
+    rows = bias.shape[0]
+    step = 64
+
+    def body(j, part):
+        a = lax.broadcasted_iota(jnp.int32, (step, rows), 0) + j * step
+        b = lax.broadcasted_iota(jnp.int32, (step, rows), 1)
+        row, key = (b, a) if transposed else (a, b)
+        bias[part, :] = jnp.where((key <= row) | (key + c * rows < prefix), 0.0, -1e30)
+
+    tiles(rows // step, step, body)
+
+
+def attend_forward(c, qkv, cross, bias, att, lse):
+    rows, d = att.shape
+    half = lane_half()
+    lane = lax.broadcasted_iota(jnp.int32, (1, PAIR), 1)
+    rt = rows // 2
+
+    def one(q, blocks):
+        scores = []
+        for keys, _, extra in blocks:
+            s = dot_nt(q, keys) * SCALE2
+            scores.append(s if extra is None else s + extra)
+        peak = functools.reduce(jnp.maximum, [jnp.max(s, -1, keepdims=True) for s in scores])
+        total = None
+        for s, (_, values, _) in zip(scores, blocks):
+            part = dot_nn(jnp.exp2(s - peak).astype(BF), values)
+            total = part if total is None else total + part
+        return total, peak
+
+    def pair(p, second):
+        cols = pl.ds(pl.multiple_of(p * PAIR, PAIR), PAIR)
+        kcols = pl.ds(pl.multiple_of(d + p * PAIR, PAIR), PAIR)
+        vcols = pl.ds(pl.multiple_of(2 * d + p * PAIR, PAIR), PAIR)
+        for r in range(2):
+            part = pl.ds(r * rt, rt)
+            results = []
+            for h in range(2):
+                mine = half == h
+                q = jnp.where(mine, qkv[part, cols], 0.0).astype(BF)
+
+                def val(v):
+                    return jnp.where(mine, v, 1.0).astype(BF)
+
+                if second:
+                    blocks = [(cross[:, cols], val(cross[:, pl.ds(pl.multiple_of(d + p * PAIR, PAIR), PAIR)]), None)]
+                    if r > 0:
+                        blocks.append((qkv[pl.ds(0, rt), kcols], val(qkv[pl.ds(0, rt), vcols]), None))
+                    blocks.append((qkv[part, kcols], val(qkv[part, vcols]), bias[part, pl.ds(r * rt, rt)]))
+                else:
+                    blocks = [(qkv[:, kcols], val(qkv[:, vcols]), bias[part, :])]
+                total, peak = one(q, blocks)
+                sums = pltpu.roll(total, HD, axis=1)
+                results.append(total / sums)
+                both = jnp.where(mine, sums, total)
+                lse[part, :] = jnp.where(lane == 2 * p + h, peak + jnp.log2(both), lse[part, :])
+            att[part, cols] = jnp.where(half == 0, results[0], results[1]).astype(BF)
+
+    for second in range(2):
+
+        @pl.when(c == second)
+        def _():
+            @pl.loop(0, d // PAIR)
+            def _(p):
+                pair(p, second == 1)
+
+
+def gelu_tile(u, a, gp, cols):
+    rows = u.shape[0]
+    step = 32
+
+    def body(j, part):
+        v = u[part, :]
+        phi = 0.5 * (1.0 + lax.erf(v * math.sqrt(0.5)))
+        dens = jnp.exp2(v * v * (-0.5 * LOG2E)) * (1.0 / math.sqrt(2.0 * math.pi))
+        a[part, cols] = (v * phi).astype(BF)
+        gp[part, cols] = (phi + v * dens).astype(BF)
+
+    tiles(rows // step, step, body)
+
+
+def forward_kernel(nz, prefix, x, par, wqkv, wout, wup, wdown, out, h1, qkv, cross, lset, att, x1, h2, a, gp, bias, lse, u, sems):
+    z, y, c, f = coords()
+    rows, d = x.shape
+    ff = wup.shape[1]
+    core = dev(z, y, 1 - c, f)
+    greet([core])
+    step = 64
+
+    def norm_one(j, part):
+        n, _ = normalise(x[part, :].astype(F32))
+        h1[part, :] = (n * par[0:1, :].astype(F32) + par[2:3, :].astype(F32)).astype(BF)
+
+    tiles(rows // step, step, norm_one)
+    fill_bias(bias, prefix[0], c, False)
+
+    def mix(j, cols):
+        qkv[:, cols] = dot_nn(h1[...], wqkv[:, cols]).astype(BF)
+
+    nq = d // TILE
+    for j in list(range(nq, 3 * nq)) + list(range(nq)):
+        mix(j, pl.ds(j * TILE, TILE))
+        if j == 3 * nq - 1:
+            pass
+    keyvals = remote(qkv.at[:, pl.ds(d, 2 * d)], cross, sems.at[0], sems.at[1], core)
+
+    @pl.when(c == 0)
+    def _():
+        keyvals.start()
+        keyvals.wait_send()
+
+    @pl.when(c == 1)
+    def _():
+        keyvals.wait_recv()
+
+    lse[...] = jnp.zeros_like(lse)
+    attend_forward(c, qkv, cross, bias, att, lse)
+    lset[...] = lse[...].T[:H, :]
+    for j in range(d // TILE):
+        cols = pl.ds(j * TILE, TILE)
+        x1[:, cols] = x[:, cols].astype(F32) + dot_nn(att[...], wout[:, cols])
+
+    def norm_two(j, part):
+        n, _ = normalise(x1[part, :])
+        h2[part, :] = (n * par[1:2, :].astype(F32) + par[3:4, :].astype(F32)).astype(BF)
+
+    tiles(rows // step, step, norm_two)
+
+    def up(j, cols):
+        u[...] = dot_nn(h2[...], wup[:, cols])
+        gelu_tile(u, a, gp, cols)
+
+    tiles(ff // TILE, TILE, up)
+
+    def down(j, cols):
+        out[:, cols] = (x1[:, cols] + dot_nn(a[...], wdown[:, cols])).astype(BF)
+
+    tiles(d // 256, 256, down)
+
+
+def run_forward(nz, prefix, x, par, wqkv, wout, wup, wdown):
+    rows, d = x.shape
+    ff = wup.shape[1]
+    S = jax.ShapeDtypeStruct
+    vm = pl.BlockSpec(memory_space=pltpu.VMEM)
+    return pl.pallas_call(
+        functools.partial(forward_kernel, nz),
+        out_shape=[
+            S((rows, d), BF), S((rows, d), BF), S((rows, 3 * d), BF), S((rows, 2 * d), BF), S((H, rows), F32),
+            S((rows, d), BF), S((rows, d), F32), S((rows, d), BF), S((rows, ff), BF), S((rows, ff), BF),
+        ],
+        in_specs=[pl.BlockSpec(memory_space=pltpu.SMEM)] + [vm] * 6,
+        out_specs=[vm] * 10,
+        scratch_shapes=[pltpu.VMEM((rows, rows), F32), pltpu.VMEM((rows, PAIR), F32), pltpu.VMEM((rows, TILE), F32), DMA((2,))],
+        compiler_params=pltpu.CompilerParams(collective_id=1, has_side_effects=True, vmem_limit_bytes=VMEM_LIMIT),
+    )(prefix, x, par, wqkv, wout, wup, wdown)
+
+
+def attend_backward(c, qkv, cross, biast, lset, deltat, go, gqkv, dcross, gq):
+    rows, d = go.shape
+    half = lane_half()
+    rt = rows // 2
+
+    def one(keys, values, q, g, lse_row, delta_row, extra):
+        s = dot_nt(keys, q) * SCALE2
+        if extra is not None:
+            s = s + extra
+        p = jnp.exp2(s - lse_row)
+        gs = (p * (dot_nt(values, g) - delta_row)).astype(BF)
+        return dot_nn(gs, q), dot_nn(p.astype(BF), g), dot_tn(gs, keys)
+
+    def pair(p, second):
+        cols = pl.ds(pl.multiple_of(p * PAIR, PAIR), PAIR)
+        kcols = pl.ds(pl.multiple_of(d + p * PAIR, PAIR), PAIR)
+        vcols = pl.ds(pl.multiple_of(2 * d + p * PAIR, PAIR), PAIR)
+        if second:
+            jobs = [(cross, cols, kcols, r * rt, rt, 0, rows, False) for r in range(2)]
+            jobs += [(qkv, kcols, vcols, 0, rt, 0, rows, True), (qkv, kcols, vcols, rt, rt, rt, rt, True)]
+        else:
+            jobs = [(qkv, kcols, vcols, r * rt, rt, 0, rows, True) for r in range(2)]
+        first = {0: True, rt: True}
+        gq[...] = jnp.zeros_like(gq)
+        for ref, kc, vc, k0, kn, q0, qn, masked in jobs:
+            gk = gv = None
+            krows, qrows = pl.ds(k0, kn), pl.ds(q0, qn)
+            keys, values = ref[krows, kc], ref[krows, vc]
+            for h in range(2):
+                mine = half == h
+                q = jnp.where(mine, qkv[qrows, cols], 0.0).astype(BF)
+                g = jnp.where(mine, go[qrows, cols], 0.0).astype(BF)
+                km = jnp.where(mine, keys, 0.0).astype(BF)
+                lse_row = lset[pl.ds(2 * p + h, 1), qrows]
+                delta_row = deltat[pl.ds(2 * p + h, 1), qrows]
+                extra = biast[krows, qrows] if masked else None
+                s = dot_nt(keys, q) * SCALE2
+                if extra is not None:
+                    s = s + extra
+                pr = jnp.exp2(s - lse_row)
+                gs = (pr * (dot_nt(values, g) - delta_row)).astype(BF)
+                k1, v1 = dot_nn(gs, q), dot_nn(pr.astype(BF), g)
+                gk, gv = (k1, v1) if gk is None else (gk + k1, gv + v1)
+                gq[qrows, :] = gq[qrows, :] + dot_tn(gs, km)
+            if ref is qkv:
+                gqkv[krows, kc] = (gk * 0.125).astype(BF)
+                gqkv[krows, vc] = gv.astype(BF)
+            else:
+                dcross[krows, kc] = (gk * 0.125).astype(BF)
+                dcross[krows, vc] = gv.astype(BF)
+        gqkv[:, cols] = (gq[...] * 0.125).astype(BF)
+
+    for second in range(2):
+
+        @pl.when(c == second)
+        def _():
+            @pl.loop(0, d // PAIR)
+            def _(p):
+                pair(p, second == 1)
+
+
+def norm_back(gh, n, scale, gain):
+    gn = gh * gain
+    return scale * (gn - jnp.mean(gn, -1, keepdims=True) - n * jnp.mean(gn * n, -1, keepdims=True))
+
+
+def backward_kernel(
+    nz, prefix, cot, par, wqkv, wout, wup, wdown, x, h1, qkv, cross, lset, att, x1, h2, a, gp,
+    grad_in, o_qkv, o_out, o_up, o_down, o_par, r_qkv, r_out, r_up, r_down, r_par,
+    wa, wb, buf, pbuf, ht, gh, gx1, gz, go, gqkv, dcross, biast, deltat, gq, acc, wsem, bsem, osem, rsem, xsem,
+):
+    z, y, c, f = coords()
+    rows, d = x.shape
+    ff = a.shape[1]
+    core = dev(z, y, 1 - c, f)
+    greet([core])
+    loads = [pltpu.make_async_copy(wdown, wa, wsem.at[0]), pltpu.make_async_copy(wup, wb, wsem.at[1])]
+    for load in loads:
+        load.start()
+
+    def emit(w, j, slot, own, land, wide):
+        if wide:
+            mine, theirs = buf.at[slot, :, :, c], buf.at[slot, :, :, 1 - c]
+            cols = pl.ds(pl.multiple_of(j * TILE, TILE), TILE)
+            to, there = own.at[:, :, :, :, cols], land.at[:, :, :, :, cols]
+        else:
+            mine, theirs = pbuf.at[slot, c], pbuf.at[slot, 1 - c]
+            to, there = own.at[j // 2, j % 2], land.at[j // 2, j % 2]
+        return (
+            pltpu.make_async_copy(mine, to, osem.at[slot]),
+            remote(theirs, there, bsem.at[slot], rsem.at[w], core),
+        )
+
+    def produce(w, count, own, land, wide, body):
+        @pl.loop(0, count)
+        def _(j):
+            slot = lax.rem(j, 2)
+
+            @pl.when(j >= 2)
+            def _():
+                local, away = emit(w, j - 2, slot, own, land, wide)
+                local.wait()
+                away.wait_send()
+
+            body(j, slot)
+            for copy in emit(w, j, slot, own, land, wide):
+                copy.start()
+
+        for j in range(count - 2, count):
+            local, away = emit(w, j, j % 2, own, land, wide)
+            local.wait()
+            away.wait_send()
+
+    gf = cot
+
+    def down(j, slot):
+        cols = pl.ds(pl.multiple_of(j * TILE, TILE), TILE)
+        pbuf[slot] = dot_tn(a[:, cols], gf[...]).astype(BF).reshape(pbuf.shape[1:])
+
+    produce(3, ff // TILE, o_down, r_down, False, down)
+    loads[0].wait()
+    ht[...] = h2[...].T
+
+    def act(j, cols):
+        gp[:, cols] = (dot_nt(gf[...], wa[cols, :]) * gp[:, cols].astype(F32)).astype(BF)
+
+    tiles(ff // TILE, TILE, act)
+    for i in range(3):
+        pltpu.make_async_copy(wqkv.at[:, pl.ds(i * d, d)], wa.at[pl.ds(i * d, d)], wsem.at[2 + i]).start()
+    pltpu.make_async_copy(wout, wa.at[pl.ds(3 * d, d)], wsem.at[5]).start()
+
+    def up(j, slot):
+        cols = pl.ds(pl.multiple_of(j * TILE, TILE), TILE)
+        buf[slot] = dot_nn(ht[...], gp[:, cols]).astype(BF).reshape(buf.shape[1:])
+
+    produce(2, ff // TILE, o_up, r_up, True, up)
+    loads[1].wait()
+    for i in range(d // 256):
+        gh[:, pl.ds(i * 256, 256)] = dot_nt(gp[...], wb[pl.ds(i * 256, 256), :])
+
+    acc[...] = jnp.zeros_like(acc)
+    step = 32
+
+    def norm_two(j, part):
+        n, scale = normalise(x1[part, :])
+        g = gh[part, :]
+        acc[1:2, :] += jnp.sum(g * n, 0, keepdims=True)
+        acc[3:4, :] += jnp.sum(g, 0, keepdims=True)
+        total = gf[part, :].astype(F32) + norm_back(g, n, scale, par[1:2, :].astype(F32))
+        gx1[part, :] = total
+        gz[part, :] = total.astype(BF)
+
+    tiles(rows // step, step, norm_two)
+    for i in range(3):
+        pltpu.make_async_copy(wqkv.at[:, pl.ds(i * d, d)], wa.at[pl.ds(i * d, d)], wsem.at[2 + i]).wait()
+    pltpu.make_async_copy(wout, wa.at[pl.ds(3 * d, d)], wsem.at[5]).wait()
+    ht[...] = att[...].T
+
+    def outp(j, slot):
+        cols = pl.ds(pl.multiple_of(j * TILE, TILE), TILE)
+        buf[slot] = dot_nn(ht[...], gz[:, cols]).astype(BF).reshape(buf.shape[1:])
+
+    produce(1, d // TILE, o_out, r_out, True, outp)
+    for i in range(d // TILE):
+        go[:, pl.ds(i * TILE, TILE)] = dot_nt(gz[...], wa[pl.ds(3 * d + i * TILE, TILE), :]).astype(BF)
+
+    fill_bias(biast, prefix[0], c, True)
+    prod = go[...].astype(F32) * att[...].astype(F32)
+    high = prod.astype(BF)
+    low = (prod - high.astype(F32)).astype(BF)
+    pick = (
+        lax.broadcasted_iota(jnp.int32, (H, d), 1) // HD == lax.broadcasted_iota(jnp.int32, (H, d), 0)
+    ).astype(BF)
+    deltat[...] = dot_nt(pick, high) + dot_nt(pick, low)
+    attend_backward(c, qkv, cross, biast, lset, deltat, go, gqkv, dcross, gq)
+    back = remote(dcross, dcross, xsem.at[0], xsem.at[1], core)
+
+    @pl.when(c == 1)
+    def _():
+        back.start()
+        back.wait_send()
+
+    @pl.when(c == 0)
+    def _():
+        back.wait_recv()
+
+        def add(j, part):
+            cols = pl.ds(d, 2 * d)
+            gqkv[part, cols] = (gqkv[part, cols].astype(F32) + dcross[part, :].astype(F32)).astype(BF)
+
+        tiles(rows // step, step, add)
+
+    ht[...] = h1[...].T
+
+    def mixed(j, slot):
+        cols = pl.ds(pl.multiple_of(j * TILE, TILE), TILE)
+        buf[slot] = dot_nn(ht[...], gqkv[:, cols]).astype(BF).reshape(buf.shape[1:])
+
+    produce(0, 3 * d // TILE, o_qkv, r_qkv, True, mixed)
+    for i in range(d // 256):
+        total = None
+        for b in range(3):
+            part = dot_nt(gqkv[:, pl.ds(b * d, d)], wa[pl.ds(b * d + i * 256, 256), :])
+            total = part if total is None else total + part
+        gh[:, pl.ds(i * 256, 256)] = total
+
+    def norm_one(j, part):
+        n, scale = normalise(x[part, :].astype(F32))
+        g = gh[part, :]
+        acc[0:1, :] += jnp.sum(g * n, 0, keepdims=True)
+        acc[2:3, :] += jnp.sum(g, 0, keepdims=True)
+        grad_in[part, :] = gx1[part, :] + norm_back(g, n, scale, par[0:1, :].astype(F32))
+
+    tiles(rows // step, step, norm_one)
+    for zy in range(d // PAIR):
+        row = acc[:, pl.ds(zy * PAIR, PAIR)].astype(BF)
+        for k in range(4):
+            buf[0, zy // 2, zy % 2, k // 2, k % 2, pl.ds(0, 16), pl.ds(0, PAIR)] = row
+    mine = buf.at[0, :, :, c, :, pl.ds(0, 16), pl.ds(0, PAIR)]
+    theirs = buf.at[0, :, :, 1 - c, :, pl.ds(0, 16), pl.ds(0, PAIR)]
+    last = (pltpu.make_async_copy(mine, o_par, osem.at[0]), remote(theirs, r_par, bsem.at[0], rsem.at[4], core))
+    for copy in last:
+        copy.start()
+    last[0].wait()
+    last[1].wait_send()
+    for w, land in enumerate((r_qkv, r_out, r_up, r_down, r_par)):
+        remote(land, land, bsem.at[0], rsem.at[w], core).wait_recv()
+
+
+def run_backward(nz, prefix, cot, par, wqkv, wout, wup, wdown, x, h1, qkv, cross, lset, att, x1, h2, a, gp):
+    rows, d = x.shape
+    ff = a.shape[1]
+    S = jax.ShapeDtypeStruct
+    vm = pl.BlockSpec(memory_space=pltpu.VMEM)
+    hbm = pl.BlockSpec(memory_space=pl.ANY)
+    V = pltpu.VMEM
+    n = nz * 8
+    halves = [S((nz, 2, 2, r, k), BF) for r, k in ((d // n, 3 * d), (d // n, d), (d // n, ff), (ff // n, d), (16, PAIR))]
+    return pl.pallas_call(
+        functools.partial(backward_kernel, nz),
+        out_shape=[S((rows, d), F32)] + halves + halves,
+        in_specs=[pl.BlockSpec(memory_space=pltpu.SMEM)] + [vm] * 2 + [hbm] * 4 + [vm] * 10,
+        out_specs=[vm] + [hbm] * 10,
+        scratch_shapes=[
+            V((ff, d), BF), V((d, ff), BF), V((2, nz, 2, 2, 2, d // n, TILE), BF), V((2, 2, 2, ff // n, d), BF),
+            V((d, rows), BF), V((rows, d), F32), V((rows, d), F32), V((rows, d), BF), V((rows, d), BF),
+            V((rows, 3 * d), BF), V((rows, 2 * d), BF), V((rows, rows), F32), V((H, rows), F32),
+            V((rows, PAIR), F32), V((16, d), F32), DMA((6,)), DMA((2,)), DMA((2,)), DMA((5,)), DMA((2,)),
+        ],
+        compiler_params=pltpu.CompilerParams(collective_id=2, has_side_effects=True, vmem_limit_bytes=VMEM_LIMIT),
+    )(prefix, cot, par, wqkv, wout, wup, wdown, x, h1, qkv, cross, lset, att, x1, h2, a, gp)
+
+
+def add_rows(dst, parts, out=None):
+    lead, r = dst.shape[:-2], dst.shape[-2]
+    out = dst if out is None else out
+    step = 16
+    count = math.prod(lead) * (r // step)
+
+    @pl.loop(0, count)
+    def _(j):
+        at = [pl.ds(pl.multiple_of(lax.rem(j, r // step) * step, step), step)]
+        rest = lax.div(j, r // step)
+        for size in reversed(lead):
+            at.insert(0, lax.rem(rest, size))
+            rest = lax.div(rest, size)
+        at = tuple(at)
+        total = dst[at].astype(F32)
+        for p in parts:
+            total = total + p[at].astype(F32)
+        out[at] = total.astype(out.dtype)
+
+
+class Scatter:
+    def __init__(self, nz, place, sums, lands, second, third, outs, sems):
+        self.nz, self.place, self.sums, self.lands = nz, place, sums, lands
+        self.second, self.third, self.outs = second, third, outs
+        self.send, self.recv = sems
+
+    @staticmethod
+    def sem_shapes(nw):
+        return [DMA((nw, 8)), DMA((nw, 8))]
+
+    def go(self, w, slot, src, dst, device):
+        return remote(src, dst, self.send.at[w, slot], self.recv.at[w, slot], device)
+
+    def zt(self, k):
+        return lax.rem(self.place[0] + k, self.nz)
+
+    def first_copy(self, w):
+        z, y, c, f = self.place
+        s, b = self.sums[w], self.second[w]
+        return (
+            self.go(w, 0, s.at[:, :, 1 - f], b, dev(z, y, c, 1 - f)),
+            self.go(w, 0, s.at[:, 1 - y], b, dev(z, 1 - y, c, f)),
+        )
+
+    def second_copies(self, w):
+        z, y, c, f = self.place
+        s, b = self.sums[w], self.third[w]
+        nz = self.nz
+        return (
+            [self.go(w, 1, s.at[:, 1 - y, f], b.at[pl.ds(0, nz)], dev(z, 1 - y, c, f))],
+            [
+                self.go(w, k, s.at[self.zt(k), y], b.at[pl.ds(2 * (k - 1), 2)], dev(self.zt(k), y, c, f))
+                for k in range(1, nz)
+            ],
+        )
+
+    def third_copies(self, w):
+        z, y, c, f = self.place
+        s, b = self.sums[w], self.third[w]
+        nz = self.nz
+        return (
+            [
+                self.go(w, 1 + k, s.at[self.zt(k), y, f], b.at[nz + k - 1], dev(self.zt(k), y, c, f))
+                for k in range(1, nz)
+            ],
+            [self.go(w, 4, s.at[z, y, 1 - f], b.at[2 * (nz - 1)], dev(z, y, c, 1 - f))],
+        )
+
+    def s1(self, w):
+        z, y, c, f = self.place
+        s, l = self.sums[w], self.lands[w]
+
+        @pl.when(c == 0)
+        def _():
+            add_rows(s.at[:, :, 1 - f], [l.at[:, :, 1 - f]])
+            self.first_copy(w)[0].start()
+            add_rows(s.at[:, :, f], [l.at[:, :, f]])
+
+        @pl.when(c == 1)
+        def _():
+            add_rows(s.at[:, 1 - y], [l.at[:, 1 - y]])
+            self.first_copy(w)[1].start()
+            add_rows(s.at[:, y], [l.at[:, y]])
+
+    def s2(self, w):
+        z, y, c, f = self.place
+        s, b = self.sums[w], self.second[w]
+
+        @pl.when(c == 0)
+        def _():
+            self.first_copy(w)[0].wait_recv()
+            add_rows(s.at[:, 1 - y, f], [b.at[:, 1 - y]])
+            for copy in self.second_copies(w)[0]:
+                copy.start()
+            add_rows(s.at[:, y, f], [b.at[:, y]])
+
+        @pl.when(c == 1)
+        def _():
+            self.first_copy(w)[1].wait_recv()
+            for k, copy in enumerate(self.second_copies(w)[1]):
+                zz = self.zt(k + 1)
+                add_rows(s.at[zz, y], [b.at[zz]])
+                copy.start()
+            add_rows(s.at[z, y], [b.at[z]])
+
+    def s3(self, w):
+        z, y, c, f = self.place
+        s, b = self.sums[w], self.third[w]
+        nz = self.nz
+
+        @pl.when(c == 0)
+        def _():
+            self.second_copies(w)[0][0].wait_recv()
+            for k, copy in enumerate(self.third_copies(w)[0]):
+                zz = self.zt(k + 1)
+                add_rows(s.at[zz, y, f], [b.at[zz]])
+                copy.start()
+            add_rows(s.at[z, y, f], [b.at[z]])
+
+        @pl.when(c == 1)
+        def _():
+            for copy in self.second_copies(w)[1]:
+                copy.wait_recv()
+            add_rows(s.at[z, y, 1 - f], [b.at[2 * k + 1 - f] for k in range(nz - 1)])
+            self.third_copies(w)[1][0].start()
+            add_rows(s.at[z, y, f], [b.at[2 * k + f] for k in range(nz - 1)])
+
+    def s4(self, w):
+        z, y, c, f = self.place
+        s, b = self.sums[w], self.third[w]
+        nz = self.nz
+
+        @pl.when(c == 0)
+        def _():
+            for copy in self.third_copies(w)[0]:
+                copy.wait_recv()
+            add_rows(s.at[z, y, f], [b.at[nz + k] for k in range(nz - 1)], self.outs[w])
+
+        @pl.when(c == 1)
+        def _():
+            self.third_copies(w)[1][0].wait_recv()
+            add_rows(s.at[z, y, f], [b.at[2 * (nz - 1)]], self.outs[w])
+
+    def finish(self, w):
+        for core in range(2):
+
+            @pl.when(self.place[2] == core)
+            def _():
+                for copy in [self.first_copy(w)[core]] + self.second_copies(w)[core] + self.third_copies(w)[core]:
+                    copy.wait_send()
+
+
+def scatter_kernel(nz, nw, *refs):
+    own, land, outs = refs[:nw], refs[nw : 2 * nw], refs[2 * nw : 3 * nw]
+    sums, lands, second, third = (refs[(3 + i) * nw : (4 + i) * nw] for i in range(4))
+    send, recv, load = refs[7 * nw :]
+    place = coords()
+    greet(all_peers(nz, *place)[:-1])
+    s = Scatter(nz, place, sums, lands, second, third, outs, (send, recv))
+    order = [3, 2, 1, 0, 4]
+    copies = {}
+    for w in order:
+        copies[w] = (
+            pltpu.make_async_copy(own[w], sums[w], load.at[w, 0]),
+            pltpu.make_async_copy(land[w], lands[w], load.at[w, 1]),
+        )
+        for copy in copies[w]:
+            copy.start()
+    for step in range(nw + 3):
+        for stage, call in enumerate((s.s1, s.s2, s.s3, s.s4)):
+            if 0 <= step - stage < nw:
+                w = order[step - stage]
+                if stage == 0:
+                    for copy in copies[w]:
+                        copy.wait()
+                call(w)
+    for w in range(nw):
+        s.finish(w)
+
+
+def scatter(nz, own, land):
+    nw = len(own)
+    V = pltpu.VMEM
+    shapes = [o.shape for o in own]
+    return pl.pallas_call(
+        functools.partial(scatter_kernel, nz, nw),
+        out_shape=[jax.ShapeDtypeStruct(s[-2:], F32) for s in shapes],
+        in_specs=[pl.BlockSpec(memory_space=pl.ANY)] * (2 * nw),
+        out_specs=[pl.BlockSpec(memory_space=pltpu.VMEM)] * nw,
+        scratch_shapes=[V(s, BF) for s in shapes]
+        + [V(s, BF) for s in shapes]
+        + [V((nz, 2) + s[-2:], BF) for s in shapes]
+        + [V((7,) + s[-2:], BF) for s in shapes]
+        + Scatter.sem_shapes(nw)
+        + [DMA((nw, 2))],
+        compiler_params=pltpu.CompilerParams(collective_id=3, has_side_effects=True, vmem_limit_bytes=VMEM_LIMIT),
+    )(*own, *land)
 
 
 def norm_rows(values, gain, shift):
@@ -118,7 +983,7 @@
     grad_branch = grad_top.astype(jnp.bfloat16)
     part_down = jnp.dot(active.T, grad_branch, preferred_element_type=jnp.float32)
     grad_active = jnp.dot(grad_branch, full_down.T, preferred_element_type=jnp.float32)
-    gelu_pull = jax.vjp(partial(jax.nn.gelu, approximate=False), hidden)[1]
+    gelu_pull = jax.vjp(functools.partial(jax.nn.gelu, approximate=False), hidden)[1]
     grad_hidden = gelu_pull(grad_active)[0].astype(jnp.bfloat16)
     part_up = jnp.dot(normed_two.T, grad_hidden, preferred_element_type=jnp.float32)
     grad_normed_two = jnp.dot(grad_hidden, full_up.T, preferred_element_type=jnp.float32)
@@ -190,31 +1055,49 @@
     )
 
 
+def exchange(array, ndp):
+    pairs = []
+    for b in range(ndp // 2):
+        pairs += [((2 * b + 1) * 2, (2 * b) * 2 + 1), ((2 * b) * 2 + 1, (2 * b + 1) * 2)]
+    moved = lax.ppermute(array, ("dp", "fsdp"), pairs)
+    stay = lax.rem(lax.axis_index("dp"), 2) == lax.axis_index("fsdp")
+    return jnp.where(stay, array, moved)
+
+
+def fast_device(ndp, frames_in, prefix_len, w_qkv, w_out, w_up, w_down, gains, shifts, cotangent):
+    nz = ndp // 4
+    d = frames_in.shape[2]
+    here = lax.axis_index("dp") * 2 + lax.axis_index("fsdp")
+    width = gains.shape[1]
+    per = PAIR // width
+    rows = jnp.concatenate([gains, shifts, jnp.zeros((12, width), BF)], 0)
+    tile = jnp.where(lax.broadcasted_iota(jnp.int32, (16, per, width), 1) == here % per, rows[:, None], 0.0)
+    tile = tile.astype(BF).reshape(16, PAIR)
+    x = exchange(frames_in[0], ndp)
+    cot = exchange(cotangent[0], ndp)
+    prefix = exchange(prefix_len, ndp)
+    full = gather(nz, (w_qkv, w_out, w_up, w_down, tile))
+    weights = [full[i].reshape(-1, full[i].shape[-1]) for i in range(4)]
+    par = full[4].reshape(d // PAIR, per, 16, PAIR).sum(1, dtype=BF).transpose(1, 0, 2).reshape(16, d)
+    result = run_forward(nz, prefix, x, par, *weights)
+    out, saved = result[0], result[1:]
+    grads = run_backward(nz, prefix, cot, par, *weights, x, *saved)
+    grad_in = exchange(grads[0], ndp)
+    owned = scatter(nz, grads[1:6], grads[6:])
+    small = lax.dynamic_slice(owned[4], (0, (here % per) * width), (16, width))
+    return (exchange(out, ndp)[None], grad_in[None]) + tuple(owned[:4]) + (small[0:2], small[2:4])
+
+
 def solution(mesh):
-    placed = (
-        P("dp", "fsdp", None),
-        P("dp"),
-        P(("dp", "fsdp"), None),
-        P(("dp", "fsdp"), None),
-        P(("dp", "fsdp"), None),
-        P(("dp", "fsdp"), None),
-        P(None, ("dp", "fsdp")),
-        P(None, ("dp", "fsdp")),
-        P("dp", "fsdp", None),
-    )
+    ndp, nf = mesh.shape["dp"], mesh.shape["fsdp"]
+    both = P(("dp", "fsdp"), None)
+    lanes = P(None, ("dp", "fsdp"))
+    block = P("dp", "fsdp", None)
+    body = functools.partial(fast_device, ndp) if (nf == 2 and ndp == 16) else on_device
     return jax.shard_map(
-        on_device,
+        body,
         mesh=mesh,
-        in_specs=placed,
-        out_specs=(
-            P("dp", "fsdp", None),
-            P("dp", "fsdp", None),
-            P(("dp", "fsdp"), None),
-            P(("dp", "fsdp"), None),
-            P(("dp", "fsdp"), None),
-            P(("dp", "fsdp"), None),
-            P(None, ("dp", "fsdp")),
-            P(None, ("dp", "fsdp")),
-        ),
+        in_specs=(block, P("dp"), both, both, both, both, lanes, lanes, block),
+        out_specs=(block, block, both, both, both, both, lanes, lanes),
         check_vma=False,
     )

time: 2000 us -> 466 us (0.23)
  waiting for transfers between devices: 1370 us -> 0.01 us
  Pallas kernels: 0 us -> 445 us
  matrix products: 407 us -> 0 us
  blocking collectives: 133 us -> 0 us
  local copies, waits for them, and re-layouts: 34.1 us -> 5.47 us
  other arithmetic: 30.8 us -> 8.47 us
    reduce_scatter x6 -> x0, waiting for transfers between devices: 1080 us -> none  [the longest x1 361 us: on_device(): lax.psum_scatter(part_down, ('dp', 'fsdp'), scatter_dimension=0, tiled=True)]
    pallas_call x0 -> x4, Pallas kernels: none -> 445 us  [the longest x1 148 us: scatter(): pl.pallas_call(functools.partial(scatter_kernel, nz, nw), out_shape=[jax....]
    dot_general x157 -> x0, matrix products: 407 us -> none  [the longest x48 90.9 us: masked_scores(): jnp.dot(query_one, key_one.T, preferred_element_type=jnp.float32) * 0.125]
    all_gather x6 -> x0, waiting for transfers between devices: 172 us -> none  [the longest x1 64.9 us: collect(): lax.all_gather(w_up, ('dp', 'fsdp'), axis=0, tiled=True)]
    all_gather x2 -> x0, blocking collectives: 133 us -> none  [the longest x1 69.8 us: collect(): lax.all_gather(shifts, ('dp', 'fsdp'), axis=1, tiled=True)]
    unnamed x16 -> x0, waiting for transfers between devices: 113 us -> none
    reduce_sum x38 -> x1, other arithmetic: 22 us -> 0.93 us  [fast_device(): full[4].reshape(d // PAIR, per, 16, PAIR).sum(1, dtype=BF)]
  transfers between devices with their start and end apart: 14 -> 5, of which waited for: 11 -> 0; matrix products, arithmetic and copies ran while one was open for 13% -> 2% of each run, Pallas kernels for 0% -> 73%
where the time goes in v1:
time: 466 us
  Pallas kernels  445 us (95%)
  other arithmetic  8.47 us (2%)
  local copies, waits for them, and re-layouts  5.47 us (1%)
  starting transfers between devices  5.06 us (1%)
    pallas_call x1, Pallas kernels, scatter(): pl.pallas_call(functools.partial(scatter_kernel, nz, nw), out_shape=[jax....  148 us
    pallas_call x1, Pallas kernels, gather(): pl.pallas_call(functools.partial(gather_kernel, nz, nw), out_shape=[jax.S...  138 us
    pallas_call x1, Pallas kernels, run_backward(): pl.pallas_call(functools.partial(backward_kernel, nz), out_shape=[S((rows...  105 us
    pallas_call x1, Pallas kernels, run_forward(): pl.pallas_call(functools.partial(forward_kernel, nz), out_shape=[S((rows,...  53.8 us
  transfers between devices with their start and end apart: 5, of which 0 were waited for; matrix products, arithmetic and copies ran while one was open for 2% of the time, Pallas kernels for 73%

profile of v1, /device:TPU:0, one launch (start us, length us, event | category | flops | bytes accessed | tf_op | source)
XLA Modules:
  0.0 465.9 jit_solution(13674287078992019954)
XLA Ops:
  0.6 0.7 collective-permute-start.1
  1.4 0.7 collective-permute-start.3
  2.1 1.2 collective-permute-start
  3.9 0.1 pad.2.clone
  4.0 0.7 maximum_maximum_fusion
  4.8 0.1 broadcast_in_dim.26
  4.9 0.1 iota.11
  4.9 0.1 iota.12
  5.0 0.6 broadcast_select_fusion.2.refs_4_
  5.6 138.2 %shard_map.152 = (bf16[4,2,2,2,32,3072]{5,4,3,2,1,0:T(8,128)(2,1)}, bf16[4,2,2,2,32,1024]{5,4,3,2,1,0:T(8,128)(2,1)}, bf16[4,2,2,2,32,4096]{5,4,3,2,1,0:T(8,128)...) custom-call(bf16[32,3072]{1,0:T(8,128)(2,1)} %refs_0_.1, bf16[32,1024]{1,0:T(8,128)(2,1)} %refs_1_.1, ...), custom_call_target="tpu_custom_call" | custom-call | tf_op jit(solution)/shard_map/pallas_call | solution.py:255
  143.8 0.9 reduce_sum.11
  144.8 0.6 copy.20
  145.4 0.0 collective-permute-done
  146.0 0.0 collective-permute-done.1
  146.0 2.3 broadcast_select_fusion.1.x
  148.3 53.8 %shard_map.153 = (bf16[512,1024]{1,0:T(8,128)(2,1)}, bf16[512,1024]{1,0:T(8,128)(2,1)}, bf16[512,3072]{1,0:T(8,128)(2,1)}, bf16[512,2048]{1,0:T(8,128)(2,1)}, f3...) custom-call(s32[1]{0:T(128)S(6)} %select_n.49.prefix, ...), custom_call_target="tpu_custom_call" | custom-call | tf_op jit(solution)/shard_map/pallas_call | solution.py:415
  202.1 0.0 collective-permute-done.3
  202.1 1.1 broadcast_select_fusion.cot
  203.2 105.0 %shard_map.154 = (f32[512,1024]{1,0:T(8,128)}, bf16[4,2,2,32,3072]{4,3,2,1,0:T(8,128)(2,1)}, bf16[4,2,2,32,1024]{4,3,2,1,0:T(8,128)(2,1)}, bf16[4,2,2,32,4096]{4...) custom-call(s32[1]{0:T(128)S(6)} %select_n.49.prefix, ...), custom_call_target="tpu_custom_call" | custom-call | tf_op jit(solution)/shard_map/pallas_call | solution.py:666
  308.1 0.8 collective-permute-start.4
  309.0 0.0 copy-done.2
  309.0 1.7 collective-permute-start.2
  310.6 148.0 %shard_map.155 = (f32[32,3072]{1,0:T(8,128)}, f32[32,1024]{1,0:T(8,128)}, f32[32,4096]{1,0:T(8,128)}, f32[128,1024]{1,0:T(8,128)}, f32[16,128]{1,0:T(8,128)}) custom-call(bf16[4,2,2,32,3072]{4,3,2,1,0:T(8,128)(2,1)} %get-tuple-element.55.refs_0_, bf16[4,2,2,32,1024]{4,3,2,1,0:T(8,128)(2,1)} %get-tuple-element.56.refs_1_, ...), custom_call_target="tpu_custom_call" | custom-call | tf_op jit(solution)/shard_map/pallas_call | solution.py:865
  458.6 1.5 fusion
  460.1 0.0 collective-permute-done.2
  460.1 1.1 select_bitcast_fusion.1
  461.2 0.0 collective-permute-done.4
  461.2 1.7 select_bitcast_fusion
  462.9 0.7 copy.26
  463.7 0.7 copy.27
  464.4 0.8 copy.28
  465.1 0.8 copy.29
  (17 shorter events, 0.1 us)
Async XLA Ops:
  0.6 145.3 %collective-permute-start.1 = (bf16[512,1024]{1,0:T(8,128)(2,1)}, bf16[512,1024]{1,0:T(8,128)(2,1)S(1)}, u32[]{:S(2)}, u32[]{:S(2)}) collective-permute-start(bf16[512,1024]{1,0:T(8,128)(2,1)} %bitcast.27), channel_id=1, source_target_pairs={{2,1},{1,2},{6,5},{5,6},{10,9},{9,10},{14,13},{13,14},{18,17},{17,... | collective-permute-start | bytes 3145736 | tf_op jit(solution)/shard_map/ppermute | solution.py:1062
  1.4 200.7 %collective-permute-start.3 = (bf16[512,1024]{1,0:T(8,128)(2,1)}, bf16[512,1024]{1,0:T(8,128)(2,1)S(1)}, u32[]{:S(2)}, u32[]{:S(2)}) collective-permute-start(bf16[512,1024]{1,0:T(8,128)(2,1)} %bitcast.28), channel_id=1, source_target_pairs={{2,1},{1,2},{6,5},{5,6},{10,9},{9,10},{14,13},{13,14},{18,17},{17,... | collective-permute-start | bytes 3145736 | tf_op jit(solution)/shard_map/ppermute | solution.py:1062
  2.1 143.3 %collective-permute-start = (s32[1]{0:T(128)}, s32[1]{0:T(128)}, u32[]{:S(2)}, u32[]{:S(2)}) collective-permute-start(s32[1]{0:T(128)} %param.10), channel_id=1, source_target_pairs={{2,1},{1,2},{6,5},{5,6},{10,9},{9,10},{14,13},{13,14},{18,17},{17,... | collective-permute-start | bytes 20 | tf_op jit(solution)/shard_map/ppermute | solution.py:1062
  148.3 53.8 %copy-start.1 = (bf16[1,512,1024]{2,1,0:T(8,128)(2,1)S(1)}, bf16[1,512,1024]{2,1,0:T(8,128)(2,1)}, u32[]{:S(2)}) copy-start(bf16[1,512,1024]{2,1,0:T(8,128)(2,1)} %param.17) | copy-start | bytes 3145732
  203.2 105.8 %copy-start.2 = (bf16[512,1024]{1,0:T(8,128)(2,1)S(1)}, bf16[512,1024]{1,0:T(8,128)(2,1)}, u32[]{:S(2)}) copy-start(bf16[512,1024]{1,0:T(8,128)(2,1)} %get-tuple-element.44) | copy-start | bytes 3145732
  308.1 153.1 %collective-permute-start.4 = (f32[512,1024]{1,0:T(8,128)}, f32[512,1024]{1,0:T(8,128)S(1)}, u32[]{:S(2)}, u32[]{:S(2)}) collective-permute-start(f32[512,1024]{1,0:T(8,128)} %get-tuple-element.54), channel_id=1, source_target_pairs={{2,1},{1,2},{6,5},{5,6},{10,9},{9,10},{14,13},{13,14},{18,17},{17,... | collective-permute-start | bytes 6291464 | tf_op jit(solution)/shard_map/ppermute | solution.py:1062
  309.0 151.1 %collective-permute-start.2 = (bf16[512,1024]{1,0:T(8,128)(2,1)S(1)}, bf16[512,1024]{1,0:T(8,128)(2,1)}, u32[]{:S(2)}, u32[]{:S(2)}) collective-permute-start(bf16[512,1024]{1,0:T(8,128)(2,1)S(1)} %copy-done.2), channel_id=1, source_target_pairs={{2,1},{1,2},{6,5},{5,6},{10,9},{9,10},{14,13},{13,14},{18,17},{17,... | collective-permute-start | bytes 3145736 | tf_op jit(solution)/shard_map/ppermute | solution.py:1062
  458.6 2.6 copy-start
  461.2 1.7 copy-start.5
  461.2 2.5 copy-start.6
  461.2 3.2 copy-start.4
  461.2 3.9 copy-start.3
